TPU v7x, 256 devices: a whole 4x4x8 slice. The times are simulated.
256 devices in a mesh: ctx: 32 (over y, z), ep: 8 (over x, core).
Axes of the slice: x: 4, y: 4, z: 8, core: 2. Of those that a mesh axis runs over, the one named last changes fastest.
Arguments:
- tokens: bfloat16 [98304, 2048], P(('ctx', 'ep')), may hold values from -6 to 6
- expert_ids: int32 [98304, 8], P(('ctx', 'ep')), may hold values from 0 to 127, as said below
- gate_codes: int32 [98304, 8], P(('ctx', 'ep')), may hold values from 4096 to 65536
- out_grad: bfloat16 [98304, 2048], P(('ctx', 'ep')), may hold values from -6 to 6
- expert_weights: bfloat16 [2048, 8, 3, 768], P('ctx', 'ep'), may hold values from -0.21875 to 0.21875
Outputs:
- moe_out: bfloat16 [98304, 2048], P(('ctx', 'ep'))
- input_grad: bfloat16 [98304, 2048], P(('ctx', 'ep'))
- weight_grads: float32 [2048, 8, 3, 768], P('ctx', 'ep')
Inputs may be any that keep to these rules, and one draw needn't show every extreme that they name: `expert_ids`: each row names 8 different experts. Within each aligned block of 384 rows (the rows of one device), every expert below 8 is named by 1 to 24 rows, and one expert below 8, the same in every block, is named by exactly 24 rows in every block.
All inputs are finite; a program needn't handle non-finite values.
Results may differ from a plain program's by a relative error of at most 0.015.
Values may be sent and summed in bfloat16 or wider, within the bound.
A program may use at most 128 MiB of HBM per device.

v0:
```python
import jax
import jax.numpy as jnp
from jax import lax
from jax.sharding import PartitionSpec as P

EXP_DEV = 1
CAP = 24


def body(tokens, expert_ids, gate_codes, out_grad, expert_weights):
    n_owner = lax.axis_size("ep")
    wave_size = n_owner * EXP_DEV
    width = tokens.shape[1]
    gates = gate_codes.astype(jnp.float32) / 65536.0
    wave_range = jnp.arange(wave_size, dtype=jnp.int32)
    chosen = expert_ids[:, :, None] == wave_range[None, None, :]
    member = jnp.any(chosen, axis=1)
    route_weight = jnp.sum(jnp.where(chosen, gates[:, :, None], 0.0), axis=1)
    position = jnp.cumsum(member.astype(jnp.int32), axis=0) - 1
    placed = member[:, :, None] & (
        position[:, :, None] == jnp.arange(CAP, dtype=jnp.int32)[None, None, :]
    )
    onehot = placed.astype(jnp.bfloat16)
    slot_rows = jnp.einsum(
        "tec,td->ecd", onehot, tokens, preferred_element_type=jnp.float32
    ).astype(jnp.bfloat16)
    slot_cotan = jnp.einsum("tec,td->ecd", onehot, out_grad, preferred_element_type=jnp.float32)
    slot_weight = jnp.sum(jnp.where(placed, route_weight[:, :, None], 0.0), axis=0)
    slot_grad = (slot_weight[:, :, None] * slot_cotan).astype(jnp.bfloat16)
    send_rows = slot_rows.reshape(n_owner, EXP_DEV, CAP, width)
    send_grad = slot_grad.reshape(n_owner, EXP_DEV, CAP, width)
    rows_in, grad_in = (
        lax.all_to_all(send_rows, "ep", split_axis=0, concat_axis=0, tiled=True),
        lax.all_to_all(send_grad, "ep", split_axis=0, concat_axis=0, tiled=True),
    )
    gathered = lax.all_gather(expert_weights, "ctx", axis=0, tiled=True)
    pre_gate = jnp.einsum(
        "sjcd,djf->sjcf", rows_in, gathered[:, :, 0, :], preferred_element_type=jnp.float32
    )
    pre_up = jnp.einsum(
        "sjcd,djf->sjcf", rows_in, gathered[:, :, 1, :], preferred_element_type=jnp.float32
    )
    soft = jax.nn.sigmoid(pre_gate)
    active = pre_gate * soft
    hidden = (active * pre_up).astype(jnp.bfloat16)
    expert_out = jnp.einsum(
        "sjcf,djf->sjcd", hidden, gathered[:, :, 2, :], preferred_element_type=jnp.float32
    ).astype(jnp.bfloat16)
    hidden_grad = jnp.einsum(
        "sjcd,djf->sjcf", grad_in, gathered[:, :, 2, :], preferred_element_type=jnp.float32
    )
    gate_grad = (hidden_grad * pre_up * soft * (1.0 + pre_gate * (1.0 - soft))).astype(jnp.bfloat16)
    up_grad = (hidden_grad * active).astype(jnp.bfloat16)
    route_input = (
        jnp.einsum(
            "sjcf,djf->sjcd", gate_grad, gathered[:, :, 0, :], preferred_element_type=jnp.float32
        )
        + jnp.einsum(
            "sjcf,djf->sjcd", up_grad, gathered[:, :, 1, :], preferred_element_type=jnp.float32
        )
    ).astype(jnp.bfloat16)
    out_back, input_back = (
        lax.all_to_all(expert_out, "ep", split_axis=0, concat_axis=0, tiled=True),
        lax.all_to_all(route_input, "ep", split_axis=0, concat_axis=0, tiled=True),
    )
    term_gate = jnp.einsum("sjcd,sjcf->djf", rows_in, gate_grad, preferred_element_type=jnp.float32)
    term_up = jnp.einsum("sjcd,sjcf->djf", rows_in, up_grad, preferred_element_type=jnp.float32)
    term_down = jnp.einsum("sjcd,sjcf->djf", grad_in, hidden, preferred_element_type=jnp.float32)
    full_terms = jnp.stack([term_gate, term_up, term_down], axis=2)
    weight_grads = lax.psum_scatter(
        full_terms.astype(jnp.bfloat16), "ctx", scatter_dimension=0, tiled=True
    ).astype(jnp.float32)
    out_back = out_back.reshape(wave_size, CAP, width)
    input_back = input_back.reshape(wave_size, CAP, width)
    combined = jnp.zeros((tokens.shape[0], width), jnp.float32)
    for expert in range(wave_size):
        picked = jnp.dot(onehot[:, expert, :], out_back[expert], preferred_element_type=jnp.float32)
        combined = combined + route_weight[:, expert : expert + 1] * picked
    input_grad = jnp.einsum("tec,ecd->td", onehot, input_back, preferred_element_type=jnp.float32)
    return (combined.astype(jnp.bfloat16), input_grad.astype(jnp.bfloat16), weight_grads)


def solution(mesh):
    placed = (
        P(("ctx", "ep"), None),
        P(("ctx", "ep"), None),
        P(("ctx", "ep"), None),
        P(("ctx", "ep"), None),
        P("ctx", "ep", None, None),
    )
    return jax.shard_map(
        body,
        mesh=mesh,
        in_specs=placed,
        out_specs=(P(("ctx", "ep"), None), P(("ctx", "ep"), None), P("ctx", "ep", None, None)),
        check_vma=False,
    )
```

profile of v0, /device:TPU:1, one launch (start us, length us, event | category | flops | bytes accessed | tf_op | source)
XLA Modules:
  0.0 425.4 jit_solution(8261615101209847765)
XLA Ops:
  7.2 0.0 all-gather.2.cloned.1.call-start
  7.2 0.7 all-gather.2.cloned.1.call-update
  7.9 0.9 fusion.42
  8.9 0.9 reduce-window.6
  9.7 0.2 slice_reduce_fusion
  10.0 0.7 convert_multiply_fusion
  10.7 0.7 select_reduce_fusion.1
  11.4 0.1 add_bitcast_fusion
  11.5 0.1 select_reduce_fusion
  11.7 1.5 fusion.16
  13.1 6.7 %all-to-all-start.2 = ((bf16[8,1,24,2048]{3,2,1,0:T(8,128)(2,1)}), bf16[8,1,24,2048]{3,2,1,0:T(8,128)(2,1)S(1)}, u32[]{:S(2)}, u32[]{:S(2)}) async-start(bf16[8,1,24,2048]{3,2,1,0:T(8,128)(2,1)} %fusion.16), calls=%async_computation.2 | async-start | bytes 1572864 | tf_op jit(solution)/shard_map/all_to_all | solution.py:34
  19.8 1.5 fusion.14
  21.3 10.8 %all-to-all-done.2 = bf16[8,1,24,2048]{3,2,1,0:T(8,128)(2,1)S(1)} async-done(((bf16[8,1,24,2048]{3,2,1,0:T(8,128)(2,1)}), bf16[8,1,24,2048]{3,2,1,0:T(8,128)(2,1)S(1)}, u32[]{:S(2)}, u32[]{:S(2)}) %all-to-all-start.2) | async-done | bytes 786464 | tf_op jit(solution)/shard_map/all_to_all | solution.py:34
  32.1 4.3 %all-to-all-start = ((bf16[8,1,24,2048]{3,2,1,0:T(8,128)(2,1)}), bf16[8,1,24,2048]{3,2,1,0:T(8,128)(2,1)S(1)}, u32[]{:S(2)}, u32[]{:S(2)}) async-start(bf16[8,1,24,2048]{3,2,1,0:T(8,128)(2,1)} %fusion.14), calls=%async_computation | async-start | bytes 1572864 | tf_op jit(solution)/shard_map/all_to_all | solution.py:33
  36.4 81.1 %all-gather.2.cloned.1.call-done = bf16[2048,1,3,768]{3,0,2,1:T(8,128)(2,1)} async-done(((bf16[64,1,3,768]{3,0,2,1:T(8,128)(2,1)}), bf16[2048,1,3,768]{3,0,2,1:T(8,128)(2,1)}) %all-gather.2.cloned.1.call-update) | async-done | bytes 9437200 | tf_op jit(solution)/shard_map/all_gather | solution.py:36
  117.6 3.5 fusion.19
  121.1 2.8 fusion.20
  123.9 2.9 fusion.31
  126.8 1.0 fusion.2
  127.9 1.0 fusion.1
  128.9 1.0 fusion
  129.9 4.1 pad_maximum_fusion
  134.0 19.3 %copy.26 = bf16[2048,1,3,768]{3,2,1,0:T(4,128)(2,1)} copy(bf16[2048,1,3,768]{0,3,2,1:T(8,128)(2,1)} %pad_maximum_fusion) | data formatting | bytes 18874368 | tf_op jit(solution)/shard_map/stack | solution.py:69
  153.4 0.0 all-reduce.3.cloned.1.call-update
  153.4 0.6 copy-done.6
  154.0 0.6 dynamic-slice
  155.3 0.1 fusion.34
  155.4 3.9 fusion.15
  159.3 5.3 %all-to-all-start.1 = ((bf16[8,1,24,2048]{3,2,1,0:T(8,128)(2,1)}), bf16[8,1,24,2048]{3,2,1,0:T(8,128)(2,1)S(1)}, u32[]{:S(2)}, u32[]{:S(2)}) async-start(bf16[8,1,24,2048]{3,2,1,0:T(8,128)(2,1)} %fusion.15), calls=%async_computation.1 | async-start | bytes 1572864 | tf_op jit(solution)/shard_map/all_to_all | solution.py:63
  164.7 3.1 fusion.3
  167.7 4.0 fusion.13
  171.8 5.2 %all-to-all-done.1 = bf16[8,1,24,2048]{3,2,1,0:T(8,128)(2,1)S(1)} async-done(((bf16[8,1,24,2048]{3,2,1,0:T(8,128)(2,1)}), bf16[8,1,24,2048]{3,2,1,0:T(8,128)(2,1)S(1)}, u32[]{:S(2)}, u32[]{:S(2)}) %all-to-all-start.1) | async-done | bytes 786464 | tf_op jit(solution)/shard_map/all_to_all | solution.py:63
  177.0 4.3 %all-to-all-start.3 = ((bf16[8,1,24,2048]{3,2,1,0:T(8,128)(2,1)}), bf16[8,1,24,2048]{3,2,1,0:T(8,128)(2,1)S(1)}, u32[]{:S(2)}, u32[]{:S(2)}) async-start(bf16[8,1,24,2048]{3,2,1,0:T(8,128)(2,1)} %fusion.13), calls=%async_computation.3 | async-start | bytes 1572864 | tf_op jit(solution)/shard_map/all_to_all | solution.py:64
  181.3 2.4 fusion.35
  183.7 2.4 fusion.36
  186.0 2.3 fusion.37
  188.3 2.4 fusion.38
  190.7 2.2 fusion.39
  192.9 2.3 fusion.40
  195.2 2.3 fusion.41
  197.6 1.8 bitcast_convert_fusion.3
  199.3 0.7 copy-done.2
  200.1 1.0 copy-done.3
  201.1 1.0 copy-done.4
  202.0 7.8 %add_convert_fusion = bf16[384,2048]{1,0:T(8,128)(2,1)} fusion(f32[384,2048]{1,0:T(8,128)S(1)} %copy-done.2, f32[384,2048]{1,0:T(8,128)S(1)} %copy-done.3, f32[384,2048]{1,0:T(8,128)S(1)} %copy-done.4, f32[384,2048]{1,0:T(8,128)} %fusion.38, f32[384,2048]{1,0:T(8,128)} %fusion.39, f32[384,2048]{1,0:T(8,128)} %fusion.40, f32[384,2048]{1,0:T(8,128)} %fusion.41, ...), kind=kOutput, calls=%fused_computation.8 | convolution fusion | flops 50331648 | bytes 23716864 | tf_op jit(solution)/shard_map/dot_general | solution.py:77
  209.8 206.2 %all-reduce.3.cloned.1.call-done = bf16[2048,1,3,768]{3,2,1,0:T(4,128)(2,1)} async-done(((bf16[2048,1,3,768]{3,2,1,0:T(4,128)(2,1)}), bf16[2048,1,3,768]{3,2,1,0:T(4,128)(2,1)}) %all-reduce.3.cloned.1.call-update) | async-done | bytes 9437200
  416.1 1.0 dynamic-slice_convert_fusion
  417.1 1.4 copy.27
  (18 shorter events, 0.1 us)
Async XLA Ops:
  7.2 4.5 %copy-start = (bf16[384,2048]{1,0:T(8,128)(2,1)S(1)}, bf16[384,2048]{1,0:T(8,128)(2,1)}, u32[]{:S(2)}) copy-start(bf16[384,2048]{1,0:T(8,128)(2,1)} %param.8) | copy-start | bytes 4718596
  7.2 12.6 %copy-start.5 = (bf16[384,2048]{1,0:T(8,128)(2,1)S(1)}, bf16[384,2048]{1,0:T(8,128)(2,1)}, u32[]{:S(2)}) copy-start(bf16[384,2048]{1,0:T(8,128)(2,1)} %param.5) | copy-start | bytes 4718596
  7.2 110.4 %all-gather.2.cloned.1.call-start = ((), (), s32[]{:S(2)}) async-start(), calls=%async_computation.4 | async-start | bytes 9732096 | tf_op jit(solution)/shard_map/all_gather | solution.py:36
  13.1 19.0 %all-to-all-start.2 = ((bf16[8,1,24,2048]{3,2,1,0:T(8,128)(2,1)}), bf16[8,1,24,2048]{3,2,1,0:T(8,128)(2,1)S(1)}, u32[]{:S(2)}, u32[]{:S(2)}) async-start(bf16[8,1,24,2048]{3,2,1,0:T(8,128)(2,1)} %fusion.16), calls=%async_computation.2 | async-start | bytes 1572864 | tf_op jit(solution)/shard_map/all_to_all | solution.py:34
  32.1 89.0 %all-to-all-start = ((bf16[8,1,24,2048]{3,2,1,0:T(8,128)(2,1)}), bf16[8,1,24,2048]{3,2,1,0:T(8,128)(2,1)S(1)}, u32[]{:S(2)}, u32[]{:S(2)}) async-start(bf16[8,1,24,2048]{3,2,1,0:T(8,128)(2,1)} %fusion.14), calls=%async_computation | async-start | bytes 1572864 | tf_op jit(solution)/shard_map/all_to_all | solution.py:33
  36.4 379.6 %all-reduce.3.cloned.1.call-start = ((), (), s32[]{:S(2)}) async-start(), calls=%async_computation.5 | async-start | bytes 25165824
  121.1 2.8 copy-start.7
  153.4 0.7 copy-start.6
  159.3 17.6 %all-to-all-start.1 = ((bf16[8,1,24,2048]{3,2,1,0:T(8,128)(2,1)}), bf16[8,1,24,2048]{3,2,1,0:T(8,128)(2,1)S(1)}, u32[]{:S(2)}, u32[]{:S(2)}) async-start(bf16[8,1,24,2048]{3,2,1,0:T(8,128)(2,1)} %fusion.15), calls=%async_computation.1 | async-start | bytes 1572864 | tf_op jit(solution)/shard_map/all_to_all | solution.py:63
  177.0 20.6 %all-to-all-start.3 = ((bf16[8,1,24,2048]{3,2,1,0:T(8,128)(2,1)}), bf16[8,1,24,2048]{3,2,1,0:T(8,128)(2,1)S(1)}, u32[]{:S(2)}, u32[]{:S(2)}) async-start(bf16[8,1,24,2048]{3,2,1,0:T(8,128)(2,1)} %fusion.13), calls=%async_computation.3 | async-start | bytes 1572864 | tf_op jit(solution)/shard_map/all_to_all | solution.py:64
  197.6 2.5 copy-start.2
  197.6 3.5 copy-start.3
  197.6 4.5 %copy-start.4 = (f32[384,2048]{1,0:T(8,128)S(1)}, f32[384,2048]{1,0:T(8,128)}, u32[]{:S(2)}) copy-start(f32[384,2048]{1,0:T(8,128)} %fusion.37) | copy-start | bytes 9437188
  202.0 216.5 %copy-start.1 = (bf16[384,2048]{1,0:T(8,128)(2,1)S(1)}, bf16[384,2048]{1,0:T(8,128)(2,1)}, u32[]{:S(2)}) copy-start(bf16[384,2048]{1,0:T(8,128)(2,1)} %param.8) | copy-start | bytes 4718596
Sparse Core Ops, SparseCore 0:
  10.6 106.9 all-gather.1
  153.5 262.5 all-reduce.2
where the time goes:
time: 427 us; the launch traced here: 425 us
  waiting for transfers between devices  304 us (71%)
  matrix products  52 us (12%)
  local copies, waits for them, and re-layouts  25 us (6%)
  starting transfers between devices  20.7 us (5%)
  between operations  14.8 us (3%)
  other arithmetic  8.73 us (2%)
    unnamed x3, waiting for transfers between devices  207 us
    all_gather x1, waiting for transfers between devices, body(): gathered = lax.all_gather(expert_weights, 'ctx', axis=0, tiled=True)  81.1 us
    dot_general x8, matrix products, body(): jnp.dot(onehot[:, expert, :], out_back[expert], preferred_element_type=jn...  24 us
    another operation x1, local copies, waits for them, and re-layouts, body(): full_terms = jnp.stack([term_gate, term_up, term_down], axis=2)  19.3 us
    all_to_all x1, waiting for transfers between devices, body(): lax.all_to_all(send_grad, 'ep', split_axis=0, concat_axis=0, tiled=True)  10.8 us
  transfers between devices with their start and end apart: 6, of which 4 were waited for; matrix products, arithmetic and copies ran while one was open for 11% of the time, Pallas kernels for 0%

commit v1 on v0

v1 whole, which is shorter than its diff:
```python
import functools

import jax
import jax.numpy as jnp
from jax import lax
from jax.experimental import pallas as pl
from jax.experimental.pallas import tpu as pltpu
from jax.sharding import PartitionSpec as P

MESH = pl.DeviceIdType.MESH
BF, F32 = jnp.bfloat16, jnp.float32
CAP = 24
PACK = 2 * CAP
LANES = 256

CUT = 112
FULL = ((0, 112), (112, 80), (112, 80))
HALF = (((0, 48), (112, 48), (112, 32)), ((48, 64), (160, 32), (144, 48)))
PLACE = (0, 112, 192)


def kernel(nx, nz, ids_ref, codes_ref, tok_hbm, og_hbm, w_hbm, moe_hbm, ig_hbm, wg_hbm,
           tok, og, wts, px, pg, pwt, slot_w, send, recv, xg, xt, pre, pre_s, pre_r,
           act, part, sum_z, sum_ya, sum_yb, back_s, back_r, moe, igr, fin_s, fin_r, wout,
           in_sem, own_s, own_r, zs, zr, yas, yar, ybs, ybr, as_, ar, es, er,
           rzs, rzr, rys, ryr, rbs, rbr, bs, br, fs, fr, out_sem):
    tokens_n = tok.shape[0]
    half_d = wts.shape[0] * 64
    ff = wts.shape[2]
    n_exp = 2 * nx
    slots = 4 * nx * CAP
    hz = nz // 2
    ctx, ep = lax.axis_index("ctx"), lax.axis_index("ep")
    y, z = lax.div(ctx, nz), lax.rem(ctx, nz)
    x, k = lax.div(ep, 2), lax.rem(ep, 2)
    h = lax.div(y, 2)
    q = lax.rem(k + h, 2)
    r = lax.rem(y + q, 2)
    other_core = (ctx, x * 2 + 1 - k)
    swap_dev = ((3 - y) * nz + z, x * 2 + 1 - k)
    y_dev = ((y + 1 - 2 * lax.rem(y, 2)) * nz + z, ep)
    z_dev = ((y * nz + lax.rem(z + 1, nz), ep), (y * nz + lax.rem(z + nz - 1, nz), ep))
    my_source = x * 4 + h * 2 + k
    my_expert = x * 2 + h

    def own(zz):
        return r * nz + lax.rem(zz + nz, nz)

    def mate(zz):
        return (1 - r) * nz + lax.rem(zz + nz, nz)

    def block(s, zz):
        return own(zz) if s < 2 else mate(zz)

    def peer(j, sign):
        dx, dh, dk = j // 4, (j // 2) % 2, j % 2
        xd = lax.rem(x + sign * dx + nx, nx)
        return xd, y + dh * (3 - 2 * y), lax.rem(h + dh, 2), lax.rem(k + dk, 2)

    def rdma(src, dst, s_sem, r_sem, dev):
        return pltpu.make_async_remote_copy(
            src_ref=src, dst_ref=dst, send_sem=s_sem, recv_sem=r_sem, device_id=dev, device_id_type=MESH
        )

    n_peer = 4 * nx
    load_tok = pltpu.make_async_copy(tok_hbm, tok, in_sem.at[0])
    load_og = pltpu.make_async_copy(og_hbm, og, in_sem.at[1])
    load_own = pltpu.make_async_copy(w_hbm, wts.at[own(z)], in_sem.at[2])
    load_tok.start()
    load_og.start()

    @pl.when(q == 0)
    def _():
        load_own.start()

    barrier = pltpu.get_barrier_semaphore()
    for j in range(1, n_peer):
        xd, yd, _, kd = peer(j, 1)
        pl.semaphore_signal(barrier, inc=1, device_id=(yd * nz + z, xd * 2 + kd), device_id_type=MESH)
    for dev in (*z_dev, y_dev):
        pl.semaphore_signal(barrier, inc=1, device_id=dev, device_id_type=MESH)
    pl.semaphore_wait(barrier, n_peer + 2)

    swap_own = rdma(w_hbm, wts.at[mate(z)], own_s, own_r, swap_dev)
    swap_in = rdma(w_hbm, wts.at[own(z)], own_s, own_r, swap_dev)

    def rows_of(d, t, s, far):
        return HALF[d][s] if t == far else FULL[s]

    def gather_z(d, t, s, arriving):
        dist = t + 1 if arriving else t
        zz = z - dist if d == 0 else z + dist
        start, count = rows_of(d, t, s, hz - 1)
        ref = wts.at[block(s, zz), pl.ds(start, count)]
        return rdma(ref, ref, zs.at[d, t, s], zr.at[d, t, s], z_dev[d])

    def gather_ya(i, arriving):
        if i == 0:
            zz, (start, count) = z, FULL[0]
        else:
            d, t = divmod(i - 1, hz)
            zz = z - 1 - t if d == 0 else z + 1 + t
            start, count = rows_of(d, t, 0, hz - 1)
        src = wts.at[mate(zz) if arriving else own(zz), pl.ds(start, count)]
        return rdma(src, src, yas.at[i], yar.at[i], y_dev)

    def gather_yb(arriving):
        ref = wts.at[mate(z) if arriving else own(z), pl.ds(*FULL[1])]
        return rdma(ref, ref, ybs, ybr, y_dev)

    def start_gather():
        for s in (0, 1):
            for d in (0, 1):
                gather_z(d, 0, s, False).start()
        gather_yb(False).start()
        gather_ya(0, False).start()

    @pl.when(q == 0)
    def _():
        load_own.wait()
        start_gather()

    @pl.when(q == 1)
    def _():
        swap_own.start()

    ids = ids_ref[...]
    gates = codes_ref[...].astype(F32) * (1.0 / 65536.0)
    member, weight = [], []
    for e in range(n_exp):
        hit = ids == e
        member.append(jnp.sum(jnp.where(hit, 1.0, 0.0), axis=0, keepdims=True))
        weight.append(jnp.sum(jnp.where(hit, gates, 0.0), axis=0, keepdims=True))
    member_all = jnp.concatenate(member, axis=0)
    before = lax.broadcasted_iota(jnp.int32, (tokens_n, tokens_n), 0)
    after = lax.broadcasted_iota(jnp.int32, (tokens_n, tokens_n), 1)
    upper = jnp.where(before <= after, 1.0, 0.0).astype(BF)
    count = jnp.dot(member_all.astype(BF), upper, preferred_element_type=F32)
    row = lax.broadcasted_iota(jnp.int32, (32, 1), 0)
    odd = k == 1
    slot_x = jnp.where(row < 16, row + 1, jnp.where(odd, jnp.where(row >= 24, row - 7, 0), jnp.where(row < 24, row + 1, 0)))
    slot_g = jnp.where(row >= 16, row - 15, jnp.where(odd, jnp.where(row < 8, row + 17, 0), jnp.where(row >= 8, row + 9, 0)))
    slot_x, slot_g = slot_x.astype(F32), slot_g.astype(F32)
    for e in range(n_exp):
        place = jnp.where(member[e] > 0.5, count[e : e + 1], -1.0)
        one_x = jnp.where(place == slot_x, 1.0, 0.0)
        one_g = jnp.where(place == slot_g, 1.0, 0.0)
        px[32 * e : 32 * e + 32, :] = one_x.astype(BF)
        pg[32 * e : 32 * e + 32, :] = one_g.astype(BF)
        slot_w[32 * e : 32 * e + 32, :] = jnp.sum(one_g * weight[e], axis=1, keepdims=True)

    @pl.when(q == 1)
    def _():
        swap_in.wait_recv()
        start_gather()

    load_tok.wait()
    load_og.wait()
    tiles = half_d // LANES

    def fill(n, carry):
        kh = lax.div(n, tiles)
        dst = pl.ds(pl.multiple_of(lax.rem(n, tiles) * LANES, LANES), LANES)
        src = pl.ds(pl.multiple_of(n * LANES, LANES), LANES)
        rows_x = jnp.dot(px[...], tok[:, src], preferred_element_type=F32)
        rows_g = jnp.dot(pg[...], og[:, src], preferred_element_type=F32) * slot_w[...]
        rows_x = rows_x.reshape(n_exp, 32, LANES)
        rows_g = rows_g.reshape(n_exp, 32, LANES)
        send[:, kh, 0:16, dst] = rows_x[:, 0:16].astype(BF)
        send[:, kh, 16:32, dst] = (rows_x[:, 16:32] + rows_g[:, 0:16]).astype(BF)
        send[:, kh, 32:48, dst] = rows_g[:, 16:32].astype(BF)
        return carry

    lax.fori_loop(0, 2 * tiles, fill, 0)

    def slots_out(j):
        xd, yd, hd, kd = peer(j, 1)
        return rdma(send.at[xd * 2 + hd, kd], recv.at[my_source], as_.at[j], ar.at[j], (yd * nz + z, xd * 2 + kd))

    def slots_in(j):
        xd, yd, hd, kd = peer(j, -1)
        ref = recv.at[xd * 4 + hd * 2 + kd]
        return rdma(ref, ref, as_.at[j], ar.at[j], (yd * nz + z, xd * 2 + kd))

    keep = pltpu.make_async_copy(send.at[my_expert, k], recv.at[my_source], as_.at[0])
    for j in range(n_peer - 1, 0, -1):
        slots_out(j).start()
    keep.start()

    for e in range(n_exp):
        at = slice(32 * e, 32 * e + 32)
        weighed = px[at, :].astype(F32) * weight[e]
        high = weighed.astype(BF).astype(F32)
        pwt[0, at, :] = high.astype(BF)
        pwt[1, at, :] = (weighed - high).astype(BF)

    gather_yb(True).wait_recv()
    for d in (0, 1):
        gather_z(d, 0, 2, False).start()

    def relay(t):
        for s in (0, 1, 2):
            for d in (0, 1):
                gather_z(d, t, s, True).wait_recv()
                if t < hz - 1:
                    gather_z(d, t + 1, s, False).start()
                if s == 0:
                    gather_ya(1 + d * hz + t, False).start()

    for t in range(hz - 1):
        relay(t)

    for j in range(1, n_peer):
        slots_in(j).wait_recv()
    keep.wait()

    def assemble(i, carry):
        at = pl.multiple_of(i * PACK, 16)
        even, uneven = recv[2 * i, 16:32, :].astype(F32), recv[2 * i + 1, 16:32, :].astype(F32)
        xg[0, pl.ds(at, 16), :] = recv[2 * i, 0:16, :]
        xg[0, pl.ds(at + 16, 16), :] = recv[2 * i + 1, 0:16, :]
        xg[0, pl.ds(at + 32, 16), :] = jnp.concatenate([even[0:8], uneven[8:16]], axis=0).astype(BF)
        xg[1, pl.ds(at, 16), :] = recv[2 * i, 32:48, :]
        xg[1, pl.ds(at + 16, 16), :] = recv[2 * i + 1, 32:48, :]
        xg[1, pl.ds(at + 32, 16), :] = jnp.concatenate([even[8:16], uneven[0:8]], axis=0).astype(BF)
        return carry

    lax.fori_loop(0, 2 * nx, assemble, 0)

    def turn(n, carry):
        at = pl.ds(pl.multiple_of(n * LANES, LANES), LANES)
        for i in (0, 1):
            xt[i, at, :] = xg[i, :, at].astype(F32).T.astype(BF)
        return carry

    lax.fori_loop(0, tiles, turn, 0)

    relay(hz - 1)
    for i in range(1 + 2 * hz):
        gather_ya(i, True).wait_recv()

    f_tiles = ff // LANES

    def swap_pre(m):
        return rdma(pre_s.at[m], pre_r.at[m], es.at[m], er.at[m], other_core)

    for m in range(3):

        def product(n, carry, m=m):
            at = pl.ds(pl.multiple_of(n * LANES, LANES), LANES)
            w = wts[:, 64 * m : 64 * m + 64, at].reshape(half_d, LANES)
            out = jnp.dot(xg[m // 2], w, preferred_element_type=F32)
            pre[m, :, at] = out
            pre_s[m, :, at] = out.astype(BF)
            return carry

        lax.fori_loop(0, f_tiles, product, 0)
        swap_pre(m).start()
    for m in range(3):
        swap_pre(m).wait_recv()

    def pointwise(n, carry):
        at = pl.ds(pl.multiple_of(n * 16, 16), 16)
        gate = pre[0, at, :] + pre_r[0, at, :].astype(F32)
        up = pre[1, at, :] + pre_r[1, at, :].astype(F32)
        grad = pre[2, at, :] + pre_r[2, at, :].astype(F32)
        soft = jax.nn.sigmoid(gate)
        active = gate * soft
        act[2, at, :] = (active * up).astype(BF)
        act[0, at, :] = (grad * up * soft * (1.0 + gate * (1.0 - soft))).astype(BF)
        act[1, at, :] = (grad * active).astype(BF)
        return carry

    lax.fori_loop(0, slots // 16, pointwise, 0)

    for m in (2, 1, 0):

        def outer(n, carry, m=m):
            at = pl.ds(pl.multiple_of(n * LANES, LANES), LANES)
            out = jnp.dot(xt[m // 2], act[m, :, at], preferred_element_type=F32)
            part[:, 64 * m : 64 * m + 64, at] = out.astype(BF).reshape(half_d // 64, 64, LANES)
            return carry

        lax.fori_loop(0, f_tiles, outer, 0)

    order = [hz] + [s * d for d in range(hz - 1, 0, -1) for s in (1, -1)] + [0]

    def reduce_ya(i):
        return rdma(part.at[mate(z + order[i]), pl.ds(0, CUT)], sum_ya.at[i], rys.at[i], ryr.at[i], y_dev)

    def reduce_z(d, t, s):
        zz = z + hz - t if d == 0 else z - hz + t
        start, count = rows_of(d, t, s, 0)
        place = PLACE[s] + start - FULL[s][0]
        return rdma(
            part.at[block(s, zz), pl.ds(start, count)],
            sum_z.at[d, t, pl.ds(place, count)],
            rzs.at[d, t, s],
            rzr.at[d, t, s],
            z_dev[d],
        )

    def add_rows(dst, src, count):
        def step(n, carry):
            at = pl.ds(pl.multiple_of(n * 16, 16), 16)
            dst[at, :] = (dst[at, :].astype(F32) + src[at, :].astype(F32)).astype(BF)
            return carry

        lax.fori_loop(0, count // 16, step, 0)

    def add_ya(i):
        reduce_ya(i).wait_recv()
        add_rows(part.at[own(z + order[i]), pl.ds(0, CUT)], sum_ya.at[i], CUT)

    def add_z(d, t, s):
        reduce_z(d, t, s).wait_recv()
        zz = z + hz - t - 1 if d == 0 else z - hz + t + 1
        start, count = rows_of(d, t, s, 0)
        place = PLACE[s] + start - FULL[s][0]
        add_rows(part.at[block(s, zz), pl.ds(start, count)], sum_z.at[d, t, pl.ds(place, count)], count)

    for i in range(2 * hz):
        reduce_ya(i).start()
    for s in (1, 2):
        for d in (0, 1):
            reduce_z(d, 0, s).start()

    def outputs(n, carry):
        rows = pl.ds(pl.multiple_of(n * (LANES // 64), LANES // 64), LANES // 64)
        at = pl.ds(pl.multiple_of(n * LANES, LANES), LANES)
        nt = (((1,), (1,)), ((), ()))
        down = wts[rows, 128:192, :].reshape(LANES, ff)
        out = lax.dot_general(act[2], down, nt, preferred_element_type=F32)
        w_gate = wts[rows, 0:64, :].reshape(LANES, ff)
        w_up = wts[rows, 64:128, :].reshape(LANES, ff)
        inp = lax.dot_general(act[0], w_gate, nt, preferred_element_type=F32)
        inp = inp + lax.dot_general(act[1], w_up, nt, preferred_element_type=F32)
        out = out.reshape(2 * nx, PACK, LANES)
        inp = inp.reshape(2 * nx, PACK, LANES)
        for i in range(2 * nx):
            back_s[2 * i, 0:16, at] = out[i, 0:16].astype(BF)
            back_s[2 * i, 16:32, at] = jnp.concatenate([out[i, 32:40], inp[i, 32:40]], axis=0).astype(BF)
            back_s[2 * i, 32:48, at] = inp[i, 0:16].astype(BF)
            back_s[2 * i + 1, 0:16, at] = out[i, 16:32].astype(BF)
            back_s[2 * i + 1, 16:32, at] = jnp.concatenate([inp[i, 40:48], out[i, 40:48]], axis=0).astype(BF)
            back_s[2 * i + 1, 32:48, at] = inp[i, 16:32].astype(BF)
        return carry

    lax.fori_loop(0, tiles, outputs, 0)

    def back_out(j):
        xd, yd, hd, kd = peer(j, 1)
        return rdma(
            back_s.at[xd * 4 + hd * 2 + kd], back_r.at[my_expert, k], bs.at[j], br.at[j], (yd * nz + z, xd * 2 + kd)
        )

    def back_in(j):
        xd, yd, hd, kd = peer(j, -1)
        ref = back_r.at[xd * 2 + hd, kd]
        return rdma(ref, ref, bs.at[j], br.at[j], (yd * nz + z, xd * 2 + kd))

    stay = pltpu.make_async_copy(back_s.at[my_source], back_r.at[my_expert, k], bs.at[0])
    for j in range(n_peer - 1, 0, -1):
        back_out(j).start()
    stay.start()

    add_ya(0)
    for d in (0, 1):
        reduce_z(d, 0, 0).start()

    def pass_on(t):
        for s in (1, 2, 0):
            for d in (0, 1):
                add_z(d, t - 1, s)
                if s == 0:
                    add_ya(1 + 2 * (t - 1) + d)
                reduce_z(d, t, s).start()

    for t in range(1, hz - 1):
        pass_on(t)

    for j in range(1, n_peer):
        back_in(j).wait_recv()
    stay.wait()

    def combine(n, carry):
        kh = lax.div(n, tiles)
        src = pl.ds(pl.multiple_of(lax.rem(n, tiles) * LANES, LANES), LANES)
        dst = pl.ds(pl.multiple_of(n * LANES, LANES), LANES)
        tn = (((0,), (0,)), ((), ()))
        rows_o = back_r[:, kh, 0:32, src].reshape(32 * n_exp, LANES)
        rows_i = back_r[:, kh, 16:48, src].reshape(32 * n_exp, LANES)
        total = lax.dot_general(pwt[0], rows_o, tn, preferred_element_type=F32)
        total = total + lax.dot_general(pwt[1], rows_o, tn, preferred_element_type=F32)
        moe[:, dst] = total.astype(BF)
        igr[:, dst] = lax.dot_general(pg[...], rows_i, tn, preferred_element_type=F32).astype(BF)
        return carry

    lax.fori_loop(0, 2 * tiles, combine, 0)
    store_moe = pltpu.make_async_copy(moe, moe_hbm, out_sem.at[0])
    store_ig = pltpu.make_async_copy(igr, ig_hbm, out_sem.at[1])
    store_moe.start()
    store_ig.start()

    pass_on(hz - 1)

    last = hz - 1
    for d in (0, 1):
        add_z(d, last, 2)
    reduce_yb = rdma(part.at[mate(z), pl.ds(*FULL[1])], sum_yb, rbs, rbr, y_dev)
    reduce_yb.start()
    reduce_ya(2 * hz - 1).wait_recv()
    for s in (1, 0):
        for d in (0, 1):
            reduce_z(d, last, s).wait_recv()
    reduce_yb.wait_recv()

    def total_rows(first, count, extra, store):
        def step(n, carry):
            at = pl.ds(pl.multiple_of(first + n * 16, 16), 16)
            near = pl.ds(pl.multiple_of(n * 16, 16), 16)
            value = part[own(z), at, :].astype(F32) + sum_z[0, last, at, :].astype(F32)
            value = value + sum_z[1, last, at, :].astype(F32) + extra[near, :].astype(F32)
            store(at, value)
            return carry

        lax.fori_loop(0, count // 16, step, 0)

    def put_out(at, value):
        wout[at, :] = value

    def put_fin(at, value):
        fin_s[at, :] = value.astype(BF)

    fin = rdma(fin_s, fin_r, fs, fr, swap_dev)

    @pl.when(q == 0)
    def _():
        total_rows(CUT, 192 - CUT, sum_yb, put_out)
        total_rows(0, CUT, sum_ya.at[2 * hz - 1], put_out)

    @pl.when(q == 1)
    def _():
        total_rows(CUT, 192 - CUT, sum_yb, put_fin)
        total_rows(0, CUT, sum_ya.at[2 * hz - 1], put_fin)
        fin.start()
        fin.wait_recv()

        def widen(n, carry):
            at = pl.ds(pl.multiple_of(n * 16, 16), 16)
            wout[at, :] = fin_r[at, :].astype(F32)
            return carry

        lax.fori_loop(0, 12, widen, 0)
        fin.wait_send()
        swap_own.wait_send()

    store_w = pltpu.make_async_copy(wout, wg_hbm, out_sem.at[2])
    store_w.start()

    for t in range(hz):
        for d in (0, 1):
            for s in (0, 1, 2):
                gather_z(d, t, s, False).wait_send()
                reduce_z(d, t, s).wait_send()
    for i in range(1 + 2 * hz):
        gather_ya(i, False).wait_send()
    gather_yb(False).wait_send()
    for i in range(2 * hz):
        reduce_ya(i).wait_send()
    reduce_yb.wait_send()
    for m in range(3):
        swap_pre(m).wait_send()
    for j in range(1, n_peer):
        slots_out(j).wait_send()
        back_out(j).wait_send()
    store_moe.wait()
    store_ig.wait()
    store_w.wait()


def layer(nx, nz, tokens, expert_ids, gate_codes, out_grad, expert_weights):
    n_tok, width = tokens.shape
    rows, _, three, ff = expert_weights.shape
    n_exp, hz, half_d = 2 * nx, nz // 2, width // 2
    blocks = 2 * nz
    slots = 4 * nx * CAP
    shard = jnp.transpose(expert_weights, (1, 2, 0, 3)).reshape(three * rows, ff)
    dma = pltpu.SemaphoreType.DMA
    vmem, hbm = pl.BlockSpec(memory_space=pltpu.VMEM), pl.BlockSpec(memory_space=pl.ANY)
    moe, input_grad, grads = pl.pallas_call(
        functools.partial(kernel, nx, nz),
        out_shape=(
            jax.ShapeDtypeStruct((n_tok, width), BF),
            jax.ShapeDtypeStruct((n_tok, width), BF),
            jax.ShapeDtypeStruct((three * rows, ff), F32),
        ),
        in_specs=[vmem, vmem, hbm, hbm, hbm],
        out_specs=(hbm, hbm, hbm),
        scratch_shapes=[
            pltpu.VMEM((n_tok, width), BF),
            pltpu.VMEM((n_tok, width), BF),
            pltpu.VMEM((blocks, 192, ff), BF),
            pltpu.VMEM((32 * n_exp, n_tok), BF),
            pltpu.VMEM((32 * n_exp, n_tok), BF),
            pltpu.VMEM((2, 32 * n_exp, n_tok), BF),
            pltpu.VMEM((32 * n_exp, 1), F32),
            pltpu.VMEM((n_exp, 2, PACK, half_d), BF),
            pltpu.VMEM((4 * nx, PACK, half_d), BF),
            pltpu.VMEM((2, slots, half_d), BF),
            pltpu.VMEM((2, half_d, slots), BF),
            pltpu.VMEM((3, slots, ff), F32),
            pltpu.VMEM((3, slots, ff), BF),
            pltpu.VMEM((3, slots, ff), BF),
            pltpu.VMEM((3, slots, ff), BF),
            pltpu.VMEM((blocks, 192, ff), BF),
            pltpu.VMEM((2, hz, 272, ff), BF),
            pltpu.VMEM((2 * hz, CUT, ff), BF),
            pltpu.VMEM((192 - CUT, ff), BF),
            pltpu.VMEM((4 * nx, PACK, half_d), BF),
            pltpu.VMEM((n_exp, 2, PACK, half_d), BF),
            pltpu.VMEM((n_tok, width), BF),
            pltpu.VMEM((n_tok, width), BF),
            pltpu.VMEM((192, ff), BF),
            pltpu.VMEM((192, ff), BF),
            pltpu.VMEM((192, ff), F32),
            dma((3,)),
            dma(()),
            dma(()),
            dma((2, hz, 3)),
            dma((2, hz, 3)),
            dma((1 + 2 * hz,)),
            dma((1 + 2 * hz,)),
            dma(()),
            dma(()),
            dma((4 * nx,)),
            dma((4 * nx,)),
            dma((3,)),
            dma((3,)),
            dma((2, hz, 3)),
            dma((2, hz, 3)),
            dma((2 * hz,)),
            dma((2 * hz,)),
            dma(()),
            dma(()),
            dma((4 * nx,)),
            dma((4 * nx,)),
            dma(()),
            dma(()),
            dma((3,)),
        ],
        compiler_params=pltpu.CompilerParams(
            collective_id=0, has_side_effects=True, vmem_limit_bytes=56 * 2**20
        ),
    )(expert_ids.T, gate_codes.T, tokens, out_grad, shard)
    grads = jnp.transpose(grads.reshape(1, three, rows, ff), (2, 0, 1, 3))
    return moe, input_grad, grads


def solution(mesh):
    nx, nz = mesh.shape["ep"] // 2, mesh.shape["ctx"] // 4
    both = P(("ctx", "ep"), None)
    weights = P("ctx", "ep", None, None)
    return jax.shard_map(
        functools.partial(layer, nx, nz),
        mesh=mesh,
        in_specs=(both, both, both, both, weights),
        out_specs=(both, both, weights),
        check_vma=False,
    )
```

time: 427 us -> 117 us (0.27)
  the two profiles are of different devices: /device:TPU:1 before, /device:TPU:35 now
where the time goes in v1:
time: 117 us; the launch traced here: 116 us
  Pallas kernels  109 us (93%)
  local copies, waits for them, and re-layouts  6.48 us (6%)
    pallas_call x1, Pallas kernels, layer(): pl.pallas_call(functools.partial(kernel, nx, nz), out_shape=(jax.ShapeDty...  109 us
    unnamed x4, local copies, waits for them, and re-layouts  3.99 us
    reshape x1, local copies, waits for them, and re-layouts, layer(): grads = jnp.transpose(grads.reshape(1, three, rows, ff), (2, 0, 1, 3))  2.49 us

profile of v1, /device:TPU:35, one launch (start us, length us, event | category | flops | bytes accessed | tf_op | source)
XLA Modules:
  0.0 116.3 jit_solution(2194767103818004573)
XLA Ops:
  0.6 109.2 %shard_map.76 = (bf16[384,2048]{1,0:T(8,128)(2,1)}, bf16[384,2048]{1,0:T(8,128)(2,1)}, f32[192,768]{1,0:T(8,128)}) custom-call(s32[8,384]{1,0:T(8,128)} %bitcast.12, s32[8,384]{1,0:T(8,128)} %bitcast.13, bf16[384,2048]{1,0:T(8,128)(2,1)} %tok_hbm.1, bf16[384,2048]{1,0:T(8,128)(2,1)} %og_hbm.1, bf16[192,768]{1,0:T(8,128)(2,1)} %bitcast.11), custom_call_target="tpu_custom_call" | custom-call | tf_op jit(solution)/shard_map/pallas_call | solution.py:491
  109.8 2.5 %copy.10 = f32[1,3,64,768]{3,0,1,2:T(1,128)} copy(f32[1,3,64,768]{3,2,1,0:T(8,128)} %bitcast.10) | data formatting | bytes 1179648 | tf_op jit(solution)/shard_map/reshape | solution.py:556
  112.3 0.0 copy-start
  112.3 2.8 %copy.13 = bf16[384,2048]{1,0:T(8,128)(2,1)} copy(bf16[384,2048]{1,0:T(8,128)(2,1)} %get-tuple-element.12) | data formatting | bytes 3145728
  115.1 0.0 copy-done
  115.1 1.1 copy.14
Async XLA Ops:
  112.3 2.9 %copy-start = (bf16[384,2048]{1,0:T(8,128)(2,1)S(1)}, bf16[384,2048]{1,0:T(8,128)(2,1)}, u32[]{:S(2)}) copy-start(bf16[384,2048]{1,0:T(8,128)(2,1)} %get-tuple-element.13) | copy-start | bytes 4718596

commit v2 on v1

v2 whole, which is shorter than its diff:
```python
import functools

import jax
import jax.numpy as jnp
from jax import lax
from jax.experimental import pallas as pl
from jax.experimental.pallas import tpu as pltpu
from jax.sharding import PartitionSpec as P

MESH = pl.DeviceIdType.MESH
BF, F32 = jnp.bfloat16, jnp.float32
CAP = 24
PACK = 2 * CAP
LANES = 256

CUT = 112
FULL = ((0, 112), (112, 80), (112, 80))
HALF = (((0, 48), (112, 48), (112, 32)), ((48, 64), (160, 32), (144, 48)))
PLACE = (0, 112, 192)


def kernel(nx, nz, ids_ref, codes_ref, tok_hbm, og_hbm, w_hbm, moe_hbm, ig_hbm, wg_hbm,
           tok, og, wts, px, pg, pwt, pgt, slot_w, send, recv, xg, xt, pre, pre_s, pre_r,
           act, part, sum_z, sum_ya, fin_z, fin_ya, fin_yb, fin_own, back_s, back_r, moe, igr, wout,
           in_sem, own_s, own_r, zs, zr, yas, yar, ybs, ybr, as_, ar, es, er,
           rzs, rzr, rys, ryr, rbs, rbr, bs, br, fs, fr, out_sem):
    tokens_n = tok.shape[0]
    half_d = wts.shape[0] * 64
    ff = wts.shape[2]
    n_exp = 2 * nx
    slots = 4 * nx * CAP
    hz = nz // 2
    ctx, ep = lax.axis_index("ctx"), lax.axis_index("ep")
    y, z = lax.div(ctx, nz), lax.rem(ctx, nz)
    x, k = lax.div(ep, 2), lax.rem(ep, 2)
    h = lax.div(y, 2)
    q = lax.rem(k + h, 2)
    r = lax.rem(y + q, 2)
    other_core = (ctx, x * 2 + 1 - k)
    swap_dev = ((3 - y) * nz + z, x * 2 + 1 - k)
    y_dev = ((y + 1 - 2 * lax.rem(y, 2)) * nz + z, ep)
    z_dev = ((y * nz + lax.rem(z + 1, nz), ep), (y * nz + lax.rem(z + nz - 1, nz), ep))
    my_source = x * 4 + h * 2 + k
    my_expert = x * 2 + h

    def own(zz):
        return r * nz + lax.rem(zz + nz, nz)

    def mate(zz):
        return (1 - r) * nz + lax.rem(zz + nz, nz)

    def block(s, zz):
        return own(zz) if s < 2 else mate(zz)

    def peer(j, sign):
        dx, dh, dk = j // 4, (j // 2) % 2, j % 2
        xd = lax.rem(x + sign * dx + nx, nx)
        return xd, y + dh * (3 - 2 * y), lax.rem(h + dh, 2), lax.rem(k + dk, 2)

    def rdma(src, dst, s_sem, r_sem, dev):
        return pltpu.make_async_remote_copy(
            src_ref=src, dst_ref=dst, send_sem=s_sem, recv_sem=r_sem, device_id=dev, device_id_type=MESH
        )

    n_peer = 4 * nx
    wide = 2 * ff // 3
    group = (pl.ds(0, wide), pl.ds(wide, ff - wide))
    group_tiles = ((0, wide // LANES), (wide // LANES, ff // LANES))
    far_y, far_k = y + q * (3 - 2 * y), k + q * (1 - 2 * k)
    y_mate = y + 1 - 2 * lax.rem(y, 2)
    home_dev = (far_y * nz + z, x * 2 + far_k)
    home_z = (
        (far_y * nz + lax.rem(z + 1, nz), x * 2 + far_k),
        (far_y * nz + lax.rem(z + nz - 1, nz), x * 2 + far_k),
    )
    home_y = ((y_mate + q * (3 - 2 * y_mate)) * nz + z, x * 2 + far_k)

    load_tok = pltpu.make_async_copy(tok_hbm, tok, in_sem.at[0])
    load_og = pltpu.make_async_copy(og_hbm, og, in_sem.at[1])

    def load_own(g):
        return pltpu.make_async_copy(w_hbm.at[:, group[g]], wts.at[own(z), :, group[g]], in_sem.at[2 + g])

    @pl.when(q == 0)
    def _():
        load_own(0).start()
        load_own(1).start()

    load_tok.start()
    load_og.start()

    barrier = pltpu.get_barrier_semaphore()
    for j in range(1, n_peer):
        xd, yd, _, kd = peer(j, 1)
        pl.semaphore_signal(barrier, inc=1, device_id=(yd * nz + z, xd * 2 + kd), device_id_type=MESH)
    cross = (
        ((3 - y) * nz + lax.rem(z + 1, nz), x * 2 + 1 - k),
        ((3 - y) * nz + lax.rem(z + nz - 1, nz), x * 2 + 1 - k),
        ((3 - y_mate) * nz + z, x * 2 + 1 - k),
    )
    for dev in (*z_dev, y_dev, *cross):
        pl.semaphore_signal(barrier, inc=1, device_id=dev, device_id_type=MESH)
    pl.semaphore_wait(barrier, n_peer + 5)

    def swap_own(g, arriving):
        dst = wts.at[own(z) if arriving else mate(z), :, group[g]]
        return rdma(w_hbm.at[:, group[g]], dst, own_s.at[g], own_r.at[g], swap_dev)

    def rows_of(d, t, s, far):
        return HALF[d][s] if t == far else FULL[s]

    def gather_z(g, d, t, s, arriving):
        dist = t + 1 if arriving else t
        zz = z - dist if d == 0 else z + dist
        start, count = rows_of(d, t, s, hz - 1)
        ref = wts.at[block(s, zz), pl.ds(start, count), group[g]]
        return rdma(ref, ref, zs.at[g, d, t, s], zr.at[g, d, t, s], z_dev[d])

    def gather_ya(g, i, arriving):
        if i == 0:
            zz, (start, count) = z, FULL[0]
        else:
            d, t = divmod(i - 1, hz)
            zz = z - 1 - t if d == 0 else z + 1 + t
            start, count = rows_of(d, t, 0, hz - 1)
        ref = wts.at[mate(zz) if arriving else own(zz), pl.ds(start, count), group[g]]
        return rdma(ref, ref, yas.at[g, i], yar.at[g, i], y_dev)

    def gather_yb(g, arriving):
        ref = wts.at[mate(z) if arriving else own(z), pl.ds(*FULL[1]), group[g]]
        return rdma(ref, ref, ybs.at[g], ybr.at[g], y_dev)

    def start_gather(g):
        for s in (0, 1):
            for d in (0, 1):
                gather_z(g, d, 0, s, False).start()
        gather_yb(g, False).start()
        gather_ya(g, 0, False).start()

    def start_mates(g):
        gather_yb(g, True).wait_recv()
        for d in (0, 1):
            gather_z(g, d, 0, 2, False).start()

    def relay(g, t, s):
        for d in (0, 1):
            gather_z(g, d, t, s, True).wait_recv()
            if t < hz - 1:
                gather_z(g, d, t + 1, s, False).start()
            if s == 0:
                gather_ya(g, 1 + d * hz + t, False).start()

    @pl.when(q == 0)
    def _():
        load_own(0).wait()
        start_gather(0)
        load_own(1).wait()

    @pl.when(q == 1)
    def _():
        swap_own(0, False).start()
        swap_own(1, False).start()

    ids = ids_ref[...]
    gates = codes_ref[...].astype(F32) * (1.0 / 65536.0)
    member, weight = [], []
    for e in range(n_exp):
        hit = ids == e
        member.append(jnp.sum(jnp.where(hit, 1.0, 0.0), axis=0, keepdims=True))
        weight.append(jnp.sum(jnp.where(hit, gates, 0.0), axis=0, keepdims=True))
    member_all = jnp.concatenate(member, axis=0)
    before = lax.broadcasted_iota(jnp.int32, (tokens_n, tokens_n), 0)
    after = lax.broadcasted_iota(jnp.int32, (tokens_n, tokens_n), 1)
    upper = jnp.where(before <= after, 1.0, 0.0).astype(BF)
    count = jnp.dot(member_all.astype(BF), upper, preferred_element_type=F32)
    row = lax.broadcasted_iota(jnp.int32, (32, 1), 0)
    odd = k == 1
    slot_x = jnp.where(row < 16, row + 1, jnp.where(odd, jnp.where(row >= 24, row - 7, 0), jnp.where(row < 24, row + 1, 0)))
    slot_g = jnp.where(row >= 16, row - 15, jnp.where(odd, jnp.where(row < 8, row + 17, 0), jnp.where(row >= 8, row + 9, 0)))
    slot_x, slot_g = slot_x.astype(F32), slot_g.astype(F32)
    for e in range(n_exp):
        place = jnp.where(member[e] > 0.5, count[e : e + 1], -1.0)
        one_x = jnp.where(place == slot_x, 1.0, 0.0)
        one_g = jnp.where(place == slot_g, 1.0, 0.0)
        px[32 * e : 32 * e + 32, :] = one_x.astype(BF)
        pg[32 * e : 32 * e + 32, :] = one_g.astype(BF)
        slot_w[32 * e : 32 * e + 32, :] = jnp.sum(one_g * weight[e], axis=1, keepdims=True)

    @pl.when(q == 1)
    def _():
        swap_own(0, True).wait_recv()
        start_gather(0)

    load_tok.wait()
    load_og.wait()
    tiles = half_d // LANES

    def fill(n, carry):
        kh = lax.div(n, tiles)
        dst = pl.ds(pl.multiple_of(lax.rem(n, tiles) * LANES, LANES), LANES)
        src = pl.ds(pl.multiple_of(n * LANES, LANES), LANES)
        rows_x = jnp.dot(px[...], tok[:, src], preferred_element_type=F32)
        rows_g = jnp.dot(pg[...], og[:, src], preferred_element_type=F32) * slot_w[...]
        rows_x = rows_x.reshape(n_exp, 32, LANES)
        rows_g = rows_g.reshape(n_exp, 32, LANES)
        send[:, kh, 0:16, dst] = rows_x[:, 0:16].astype(BF)
        send[:, kh, 16:32, dst] = (rows_x[:, 16:32] + rows_g[:, 0:16]).astype(BF)
        send[:, kh, 32:48, dst] = rows_g[:, 16:32].astype(BF)
        return carry

    lax.fori_loop(0, 2 * tiles, fill, 0)

    def slots_out(j):
        xd, yd, hd, kd = peer(j, 1)
        return rdma(send.at[xd * 2 + hd, kd], recv.at[my_source], as_.at[j], ar.at[j], (yd * nz + z, xd * 2 + kd))

    def slots_in(j):
        xd, yd, hd, kd = peer(j, -1)
        ref = recv.at[xd * 4 + hd * 2 + kd]
        return rdma(ref, ref, as_.at[j], ar.at[j], (yd * nz + z, xd * 2 + kd))

    keep = pltpu.make_async_copy(send.at[my_expert, k], recv.at[my_source], as_.at[0])
    for j in range(n_peer - 1, 0, -1):
        slots_out(j).start()
    keep.start()

    start_mates(0)

    for e in range(0, n_exp, 4):
        weighed = jnp.concatenate(
            [px[32 * i : 32 * i + 32, :].astype(F32) * weight[i] for i in range(e, min(e + 4, n_exp))], axis=0
        )
        at = slice(32 * e, 32 * e + weighed.shape[0])
        weighed = weighed.T
        high = weighed.astype(BF)
        pwt[0, :, at] = high
        pwt[1, :, at] = (weighed - high.astype(F32)).astype(BF)
        pgt[:, at] = pg[at, :].astype(F32).T.astype(BF)

    def assemble(i, carry):
        at = pl.multiple_of(i * PACK, 16)
        even, uneven = recv[2 * i, 16:32, :].astype(F32), recv[2 * i + 1, 16:32, :].astype(F32)
        xg[0, pl.ds(at, 16), :] = recv[2 * i, 0:16, :]
        xg[0, pl.ds(at + 16, 16), :] = recv[2 * i + 1, 0:16, :]
        xg[0, pl.ds(at + 32, 16), :] = jnp.concatenate([even[0:8], uneven[8:16]], axis=0).astype(BF)
        xg[1, pl.ds(at, 16), :] = recv[2 * i, 32:48, :]
        xg[1, pl.ds(at + 16, 16), :] = recv[2 * i + 1, 32:48, :]
        xg[1, pl.ds(at + 32, 16), :] = jnp.concatenate([even[8:16], uneven[0:8]], axis=0).astype(BF)
        return carry

    def turn(first, end):
        def step(n, carry):
            at = pl.ds(pl.multiple_of(n * LANES, LANES), LANES)
            for i in (0, 1):
                xt[i, at, :] = xg[i, :, at].astype(F32).T.astype(BF)
            return carry

        lax.fori_loop(first, end, step, 0)

    def swap_pre(g, m):
        return rdma(
            pre_s.at[m, :, group[g]], pre_r.at[m, :, group[g]], es.at[g, m], er.at[g, m], other_core
        )

    def product(g, m):
        def step(n, carry):
            at = pl.ds(pl.multiple_of(n * LANES, LANES), LANES)
            w = wts[:, 64 * m : 64 * m + 64, at].reshape(half_d, LANES)
            out = jnp.dot(xg[m // 2], w, preferred_element_type=F32)
            pre[m, :, at] = out
            pre_s[m, :, at] = out.astype(BF)
            return carry

        lax.fori_loop(*group_tiles[g], step, 0)
        swap_pre(g, m).start()

    def pointwise(g):
        for m in range(3):
            swap_pre(g, m).wait_recv()

        def step(n, carry):
            at = pl.ds(pl.multiple_of(n * 16, 16), 16)
            gate = pre[0, at, group[g]] + pre_r[0, at, group[g]].astype(F32)
            up = pre[1, at, group[g]] + pre_r[1, at, group[g]].astype(F32)
            grad = pre[2, at, group[g]] + pre_r[2, at, group[g]].astype(F32)
            soft = jax.nn.sigmoid(gate)
            active = gate * soft
            act[2, at, group[g]] = (active * up).astype(BF)
            act[0, at, group[g]] = (grad * up * soft * (1.0 + gate * (1.0 - soft))).astype(BF)
            act[1, at, group[g]] = (grad * active).astype(BF)
            return carry

        lax.fori_loop(0, slots // 16, step, 0)

    def outer(g, m):
        def step(n, carry):
            at = pl.ds(pl.multiple_of(n * LANES, LANES), LANES)
            out = jnp.dot(xt[m // 2], act[m, :, at], preferred_element_type=F32)
            part[:, 64 * m : 64 * m + 64, at] = out.astype(BF).reshape(half_d // 64, 64, LANES)
            return carry

        lax.fori_loop(*group_tiles[g], step, 0)

    order = [hz] + [s * d for d in range(hz - 1, 0, -1) for s in (1, -1)] + [0]
    last = hz - 1

    def reduce_ya(g, i):
        src = part.at[mate(z + order[i]), pl.ds(0, CUT), group[g]]
        if order[i] == 0:
            return rdma(src, fin_ya.at[:, group[g]], rys.at[g, i], ryr.at[g, i], home_y)
        return rdma(src, sum_ya.at[i, :, group[g]], rys.at[g, i], ryr.at[g, i], y_dev)

    def reduce_yb(g):
        return rdma(
            part.at[mate(z), pl.ds(*FULL[1]), group[g]], fin_yb.at[:, group[g]], rbs.at[g], rbr.at[g], home_y
        )

    def reduce_own(g):
        return rdma(part.at[own(z), :, group[g]], fin_own.at[:, group[g]], fs.at[g], fr.at[g], home_dev)

    def reduce_z(g, d, t, s):
        zz = z + hz - t if d == 0 else z - hz + t
        start, count = rows_of(d, t, s, 0)
        place = PLACE[s] + start - FULL[s][0]
        src = part.at[block(s, zz), pl.ds(start, count), group[g]]
        if t == last and s < 2:
            dst, dev = fin_z.at[d, pl.ds(start, count), group[g]], home_z[d]
        else:
            dst, dev = sum_z.at[d, t, pl.ds(place, count), group[g]], z_dev[d]
        return rdma(src, dst, rzs.at[g, d, t, s], rzr.at[g, d, t, s], dev)

    def add_rows(dst, src, count, g):
        dst[:, group[g]] = dst[:, group[g]] + src[:, group[g]]

    def add_ya(g, i):
        reduce_ya(g, i).wait_recv()
        add_rows(part.at[own(z + order[i]), pl.ds(0, CUT)], sum_ya.at[i], CUT, g)

    def add_z(g, d, t, s):
        reduce_z(g, d, t, s).wait_recv()
        zz = z + hz - t - 1 if d == 0 else z - hz + t + 1
        start, count = rows_of(d, t, s, 0)
        place = PLACE[s] + start - FULL[s][0]
        add_rows(part.at[block(s, zz), pl.ds(start, count)], sum_z.at[d, t, pl.ds(place, count)], count, g)

    def start_reduce(g):
        for i in range(2 * hz):
            reduce_ya(g, i).start()
        for s in (1, 2):
            for d in (0, 1):
                reduce_z(g, d, 0, s).start()

        @pl.when(q == 1)
        def _():
            reduce_own(g).start()

    def start_far(g):
        add_ya(g, 0)
        for d in (0, 1):
            reduce_z(g, d, 0, 0).start()

    def pass_on(g, t, s):
        for d in (0, 1):
            add_z(g, d, t - 1, s)
            if s == 0:
                add_ya(g, 1 + 2 * (t - 1) + d)
            reduce_z(g, d, t, s).start()

    def finish_mates(g):
        for d in (0, 1):
            add_z(g, d, last, 2)
        reduce_yb(g).start()

    def finish(g):
        reduce_ya(g, 2 * hz - 1).wait_recv()
        for s in (1, 0):
            for d in (0, 1):
                reduce_z(g, d, last, s).wait_recv()
        reduce_yb(g).wait_recv()
        lane_tiles = ff // 128
        first = group_tiles[g][0] * (LANES // 128)

        def total_rows(mine, start, count, extra):
            def step(n, carry):
                at = pl.ds(pl.multiple_of(start + n * 16, 16), 16)
                near = pl.ds(pl.multiple_of(n * 16, 16), 16)
                value = mine[at, group[g]].astype(F32) + fin_z[0, at, group[g]].astype(F32)
                value = value + fin_z[1, at, group[g]].astype(F32) + extra[near, group[g]].astype(F32)
                piece = start // 16 + n
                base = lax.rem(piece, 4) * 16 * 3 * lane_tiles + lax.div(piece, 4) * lane_tiles
                for i in range(value.shape[1] // 128):
                    wout[pl.ds(base + first + i, 16, stride=3 * lane_tiles), :] = value[:, 128 * i : 128 * i + 128]
                return carry

            lax.fori_loop(0, count // 16, step, 0)

        @pl.when(q == 0)
        def _():
            total_rows(part.at[own(z)], CUT, 192 - CUT, fin_yb)
            total_rows(part.at[own(z)], 0, CUT, fin_ya)

        @pl.when(q == 1)
        def _():
            reduce_own(g).wait_recv()
            total_rows(fin_own, CUT, 192 - CUT, fin_yb)
            total_rows(fin_own, 0, CUT, fin_ya)

    def outputs(first, end):
        def step(n, carry):
            rows = pl.ds(pl.multiple_of(n * (LANES // 64), LANES // 64), LANES // 64)
            at = pl.ds(pl.multiple_of(n * LANES, LANES), LANES)
            nt = (((1,), (1,)), ((), ()))
            down = wts[rows, 128:192, :].reshape(LANES, ff)
            out = lax.dot_general(act[2], down, nt, preferred_element_type=F32)
            w_gate = wts[rows, 0:64, :].reshape(LANES, ff)
            w_up = wts[rows, 64:128, :].reshape(LANES, ff)
            inp = lax.dot_general(act[0], w_gate, nt, preferred_element_type=F32)
            inp = inp + lax.dot_general(act[1], w_up, nt, preferred_element_type=F32)
            out = out.reshape(2 * nx, PACK, LANES)
            inp = inp.reshape(2 * nx, PACK, LANES)
            for i in range(2 * nx):
                back_s[2 * i, 0:16, at] = out[i, 0:16].astype(BF)
                back_s[2 * i, 16:32, at] = jnp.concatenate([out[i, 32:40], inp[i, 32:40]], axis=0).astype(BF)
                back_s[2 * i, 32:48, at] = inp[i, 0:16].astype(BF)
                back_s[2 * i + 1, 0:16, at] = out[i, 16:32].astype(BF)
                back_s[2 * i + 1, 16:32, at] = jnp.concatenate([inp[i, 40:48], out[i, 40:48]], axis=0).astype(BF)
                back_s[2 * i + 1, 32:48, at] = inp[i, 16:32].astype(BF)
            return carry

        lax.fori_loop(first, end, step, 0)

    def back_out(j):
        xd, yd, hd, kd = peer(j, 1)
        return rdma(
            back_s.at[xd * 4 + hd * 2 + kd], back_r.at[my_expert, k], bs.at[j], br.at[j], (yd * nz + z, xd * 2 + kd)
        )

    def back_in(j):
        xd, yd, hd, kd = peer(j, -1)
        ref = back_r.at[xd * 2 + hd, kd]
        return rdma(ref, ref, bs.at[j], br.at[j], (yd * nz + z, xd * 2 + kd))

    stay = pltpu.make_async_copy(back_s.at[my_source], back_r.at[my_expert, k], bs.at[0])

    def combine(n, carry):
        kh = lax.div(n, tiles)
        src = pl.ds(pl.multiple_of(lax.rem(n, tiles) * LANES, LANES), LANES)
        dst = pl.ds(pl.multiple_of(n * LANES, LANES), LANES)
        rows_o = back_r[:, kh, 0:32, src].reshape(32 * n_exp, LANES)
        rows_i = back_r[:, kh, 16:48, src].reshape(32 * n_exp, LANES)
        total = jnp.dot(pwt[0], rows_o, preferred_element_type=F32)
        total = total + jnp.dot(pwt[1], rows_o, preferred_element_type=F32)
        moe[:, dst] = total.astype(BF)
        igr[:, dst] = jnp.dot(pgt[...], rows_i, preferred_element_type=F32).astype(BF)
        return carry

    for t in range(hz - 1):
        for s in (0, 1, 2):
            relay(0, t, s)

    @pl.when(q == 1)
    def _():
        swap_own(1, True).wait_recv()

    start_gather(1)
    for s in (0, 1, 2):
        relay(0, hz - 1, s)
    start_mates(1)
    for j in range(1, n_peer):
        slots_in(j).wait_recv()
    keep.wait()
    lax.fori_loop(0, 2 * nx, assemble, 0)
    for i in range(1 + 2 * hz):
        gather_ya(0, i, True).wait_recv()

    work = [functools.partial(product, 0, m) for m in range(3)]
    work += [functools.partial(turn, 0, tiles // 2), functools.partial(turn, tiles // 2, tiles)]
    work += [functools.partial(pointwise, 0)] + [functools.partial(outer, 0, m) for m in (2, 1, 0)]
    relays = [functools.partial(relay, 1, t, s) for t in range(hz) for s in (0, 1, 2)]
    while work or relays:
        if work:
            work.pop(0)()
        if relays:
            relays.pop(0)()

    start_reduce(0)
    for i in range(1 + 2 * hz):
        gather_ya(1, i, True).wait_recv()
    for m in range(3):
        product(1, m)
    start_far(0)
    pointwise(1)
    work = [functools.partial(outputs, n, n + 1) for n in range(tiles)]
    work += [lambda: [back_out(j).start() for j in range(n_peer - 1, 0, -1)] + [stay.start()]]
    work += [functools.partial(outer, 1, m) for m in (2, 1, 0)]
    sums = [functools.partial(pass_on, 0, t, s) for t in range(1, hz) for s in (1, 2, 0)]
    while work or sums:
        if sums:
            sums.pop(0)()
        if work:
            work.pop(0)()

    start_reduce(1)
    finish_mates(0)
    start_far(1)
    for t in range(1, hz):
        for s in (1, 2, 0):
            pass_on(1, t, s)
    finish_mates(1)

    for j in range(1, n_peer):
        back_in(j).wait_recv()
    stay.wait()
    lax.fori_loop(0, 2 * tiles, combine, 0)
    store_moe = pltpu.make_async_copy(moe, moe_hbm, out_sem.at[0])
    store_ig = pltpu.make_async_copy(igr, ig_hbm, out_sem.at[1])
    store_moe.start()
    store_ig.start()
    finish(0)
    finish(1)
    store_w = pltpu.make_async_copy(wout, wg_hbm, out_sem.at[2])
    store_w.start()

    for g in (0, 1):
        for t in range(hz):
            for d in (0, 1):
                for s in (0, 1, 2):
                    gather_z(g, d, t, s, False).wait_send()
                    reduce_z(g, d, t, s).wait_send()
        for i in range(1 + 2 * hz):
            gather_ya(g, i, False).wait_send()
        gather_yb(g, False).wait_send()
        for i in range(2 * hz):
            reduce_ya(g, i).wait_send()
        reduce_yb(g).wait_send()
        for m in range(3):
            swap_pre(g, m).wait_send()

    @pl.when(q == 1)
    def _():
        for g in (0, 1):
            swap_own(g, False).wait_send()
            reduce_own(g).wait_send()

    for j in range(1, n_peer):
        slots_out(j).wait_send()
        back_out(j).wait_send()
    store_moe.wait()
    store_ig.wait()
    store_w.wait()


def layer(nx, nz, tokens, expert_ids, gate_codes, out_grad, expert_weights):
    n_tok, width = tokens.shape
    rows, _, three, ff = expert_weights.shape
    n_exp, hz, half_d = 2 * nx, nz // 2, width // 2
    blocks = 2 * nz
    slots = 4 * nx * CAP
    shard = jnp.transpose(expert_weights, (1, 2, 0, 3)).reshape(three * rows, ff)
    dma = pltpu.SemaphoreType.DMA
    vmem, hbm = pl.BlockSpec(memory_space=pltpu.VMEM), pl.BlockSpec(memory_space=pl.ANY)
    moe, input_grad, grads = pl.pallas_call(
        functools.partial(kernel, nx, nz),
        out_shape=(
            jax.ShapeDtypeStruct((n_tok, width), BF),
            jax.ShapeDtypeStruct((n_tok, width), BF),
            jax.ShapeDtypeStruct((three * rows * ff // 128, 128), F32),
        ),
        in_specs=[vmem, vmem, hbm, hbm, hbm],
        out_specs=(hbm, hbm, hbm),
        scratch_shapes=[
            pltpu.VMEM((n_tok, width), BF),
            pltpu.VMEM((n_tok, width), BF),
            pltpu.VMEM((blocks, 192, ff), BF),
            pltpu.VMEM((32 * n_exp, n_tok), BF),
            pltpu.VMEM((32 * n_exp, n_tok), BF),
            pltpu.VMEM((2, n_tok, 32 * n_exp), BF),
            pltpu.VMEM((n_tok, 32 * n_exp), BF),
            pltpu.VMEM((32 * n_exp, 1), F32),
            pltpu.VMEM((n_exp, 2, PACK, half_d), BF),
            pltpu.VMEM((4 * nx, PACK, half_d), BF),
            pltpu.VMEM((2, slots, half_d), BF),
            pltpu.VMEM((2, half_d, slots), BF),
            pltpu.VMEM((3, slots, ff), F32),
            pltpu.VMEM((3, slots, ff), BF),
            pltpu.VMEM((3, slots, ff), BF),
            pltpu.VMEM((3, slots, ff), BF),
            pltpu.VMEM((blocks, 192, ff), BF),
            pltpu.VMEM((2, hz, 272, ff), BF),
            pltpu.VMEM((2 * hz, CUT, ff), BF),
            pltpu.VMEM((2, 192, ff), BF),
            pltpu.VMEM((CUT, ff), BF),
            pltpu.VMEM((192 - CUT, ff), BF),
            pltpu.VMEM((192, ff), BF),
            pltpu.VMEM((4 * nx, PACK, half_d), BF),
            pltpu.VMEM((n_exp, 2, PACK, half_d), BF),
            pltpu.VMEM((n_tok, width), BF),
            pltpu.VMEM((n_tok, width), BF),
            pltpu.VMEM((192 * ff // 128, 128), F32),
            dma((4,)),
            dma((2,)),
            dma((2,)),
            dma((2, 2, hz, 3)),
            dma((2, 2, hz, 3)),
            dma((2, 1 + 2 * hz)),
            dma((2, 1 + 2 * hz)),
            dma((2,)),
            dma((2,)),
            dma((4 * nx,)),
            dma((4 * nx,)),
            dma((2, 3)),
            dma((2, 3)),
            dma((2, 2, hz, 3)),
            dma((2, 2, hz, 3)),
            dma((2, 2 * hz)),
            dma((2, 2 * hz)),
            dma((2,)),
            dma((2,)),
            dma((4 * nx,)),
            dma((4 * nx,)),
            dma((2,)),
            dma((2,)),
            dma((3,)),
        ],
        compiler_params=pltpu.CompilerParams(
            collective_id=0, has_side_effects=True, vmem_limit_bytes=56 * 2**20
        ),
    )(expert_ids.T, gate_codes.T, tokens, out_grad, shard)
    return moe, input_grad, grads.reshape(rows, 1, three, ff)


def solution(mesh):
    nx, nz = mesh.shape["ep"] // 2, mesh.shape["ctx"] // 4
    both = P(("ctx", "ep"), None)
    weights = P("ctx", "ep", None, None)
    return jax.shard_map(
        functools.partial(layer, nx, nz),
        mesh=mesh,
        in_specs=(both, both, both, both, weights),
        out_specs=(both, both, weights),
        check_vma=False,
    )
```

time: 117 us -> 109 us (0.932)
  the two profiles are of different devices: /device:TPU:35 before, /device:TPU:1 now
where the time goes in v2:
time: 109 us
  Pallas kernels  103 us (94%)
  local copies, waits for them, and re-layouts  5.13 us (5%)
    pallas_call x1, Pallas kernels, layer(): pl.pallas_call(functools.partial(kernel, nx, nz), out_shape=(jax.ShapeDty...  103 us
    unnamed x7, local copies, waits for them, and re-layouts  5.13 us

profile of v2, /device:TPU:1, one launch (start us, length us, event | category | flops | bytes accessed | tf_op | source)
XLA Modules:
  0.0 108.5 jit_solution(5357996813691870801)
XLA Ops:
  0.6 102.8 %shard_map.76 = (bf16[384,2048]{1,0:T(8,128)(2,1)}, bf16[384,2048]{1,0:T(8,128)(2,1)}, f32[1152,128]{1,0:T(8,128)}) custom-call(s32[8,384]{1,0:T(8,128)} %bitcast.8, s32[8,384]{1,0:T(8,128)} %bitcast.9, bf16[384,2048]{1,0:T(8,128)(2,1)} %tok_hbm.1, bf16[384,2048]{1,0:T(8,128)(2,1)} %og_hbm.1, bf16[192,768]{1,0:T(8,128)(2,1)} %bitcast.7), custom_call_target="tpu_custom_call" | custom-call | tf_op jit(solution)/shard_map/pallas_call | solution.py:562
  103.4 0.0 copy-start
  103.4 2.8 %copy.13 = bf16[384,2048]{1,0:T(8,128)(2,1)} copy(bf16[384,2048]{1,0:T(8,128)(2,1)} %get-tuple-element.18) | data formatting | bytes 3145728
  106.3 0.0 copy-done
  106.3 0.0 copy-start.1
  106.3 1.1 %copy.14 = bf16[384,2048]{1,0:T(8,128)(2,1)} copy(bf16[384,2048]{1,0:T(8,128)(2,1)S(1)} %copy-done) | data formatting | bytes 3145728
  107.4 0.3 copy-done.1
  107.7 0.8 copy.15
Async XLA Ops:
  103.4 2.9 %copy-start = (bf16[384,2048]{1,0:T(8,128)(2,1)S(1)}, bf16[384,2048]{1,0:T(8,128)(2,1)}, u32[]{:S(2)}) copy-start(bf16[384,2048]{1,0:T(8,128)(2,1)} %get-tuple-element.19) | copy-start | bytes 4718596
  106.3 1.5 %copy-start.1 = (f32[1152,128]{1,0:T(8,128)S(1)}, f32[1152,128]{1,0:T(8,128)}, u32[]{:S(2)}) copy-start(f32[1152,128]{1,0:T(8,128)} %get-tuple-element.8) | copy-start | bytes 1769476

commit v3 on v2

--- a/solution.py
+++ b/solution.py
@@ -19,11 +19,11 @@
 PLACE = (0, 112, 192)
 
 
-def kernel(nx, nz, ids_ref, codes_ref, tok_hbm, og_hbm, w_hbm, moe_hbm, ig_hbm, wg_hbm,
+def kernel(nx, nz, ids_ref, codes_ref, tok_hbm, og_hbm, w_hbm, moe, igr, wout,
            tok, og, wts, px, pg, pwt, pgt, slot_w, send, recv, xg, xt, pre, pre_s, pre_r,
-           act, part, sum_z, sum_ya, fin_z, fin_ya, fin_yb, fin_own, back_s, back_r, moe, igr, wout,
+           act, part, sum_z, sum_ya, fin_z, fin_ya, fin_yb, fin_own, back_s, back_r,
            in_sem, own_s, own_r, zs, zr, yas, yar, ybs, ybr, as_, ar, es, er,
-           rzs, rzr, rys, ryr, rbs, rbr, bs, br, fs, fr, out_sem):
+           rzs, rzr, rys, ryr, rbs, rbr, bs, br, fs, fr):
     tokens_n = tok.shape[0]
     half_d = wts.shape[0] * 64
     ff = wts.shape[2]
@@ -488,38 +488,37 @@
         gather_ya(1, i, True).wait_recv()
     for m in range(3):
         product(1, m)
+    pass_on(0, 1, 1)
+    pass_on(0, 1, 2)
+    pointwise(1)
     start_far(0)
-    pointwise(1)
-    work = [functools.partial(outputs, n, n + 1) for n in range(tiles)]
-    work += [lambda: [back_out(j).start() for j in range(n_peer - 1, 0, -1)] + [stay.start()]]
-    work += [functools.partial(outer, 1, m) for m in (2, 1, 0)]
-    sums = [functools.partial(pass_on, 0, t, s) for t in range(1, hz) for s in (1, 2, 0)]
-    while work or sums:
-        if sums:
-            sums.pop(0)()
-        if work:
-            work.pop(0)()
-
+    for m in (2, 1, 0):
+        outer(1, m)
     start_reduce(1)
+    outputs(0, tiles)
+    for j in range(n_peer - 1, 0, -1):
+        back_out(j).start()
+    stay.start()
+    for t in range(1, hz):
+        if t + 1 < hz:
+            pass_on(0, t + 1, 1)
+            pass_on(0, t + 1, 2)
+        pass_on(0, t, 0)
+        pass_on(1, t, 1)
+        pass_on(1, t, 2)
     finish_mates(0)
     start_far(1)
     for t in range(1, hz):
-        for s in (1, 2, 0):
-            pass_on(1, t, s)
-    finish_mates(1)
+        if t == hz - 1:
+            finish_mates(1)
+        pass_on(1, t, 0)
 
     for j in range(1, n_peer):
         back_in(j).wait_recv()
     stay.wait()
     lax.fori_loop(0, 2 * tiles, combine, 0)
-    store_moe = pltpu.make_async_copy(moe, moe_hbm, out_sem.at[0])
-    store_ig = pltpu.make_async_copy(igr, ig_hbm, out_sem.at[1])
-    store_moe.start()
-    store_ig.start()
     finish(0)
     finish(1)
-    store_w = pltpu.make_async_copy(wout, wg_hbm, out_sem.at[2])
-    store_w.start()
 
     for g in (0, 1):
         for t in range(hz):
@@ -545,9 +544,6 @@
     for j in range(1, n_peer):
         slots_out(j).wait_send()
         back_out(j).wait_send()
-    store_moe.wait()
-    store_ig.wait()
-    store_w.wait()
 
 
 def layer(nx, nz, tokens, expert_ids, gate_codes, out_grad, expert_weights):
@@ -562,12 +558,12 @@
     moe, input_grad, grads = pl.pallas_call(
         functools.partial(kernel, nx, nz),
         out_shape=(
-            jax.ShapeDtypeStruct((n_tok, width), BF),
-            jax.ShapeDtypeStruct((n_tok, width), BF),
-            jax.ShapeDtypeStruct((three * rows * ff // 128, 128), F32),
+            pltpu.VMEM((n_tok, width), BF),
+            pltpu.VMEM((n_tok, width), BF),
+            pltpu.VMEM((three * rows * ff // 128, 128), F32),
         ),
         in_specs=[vmem, vmem, hbm, hbm, hbm],
-        out_specs=(hbm, hbm, hbm),
+        out_specs=(vmem, vmem, vmem),
         scratch_shapes=[
             pltpu.VMEM((n_tok, width), BF),
             pltpu.VMEM((n_tok, width), BF),
@@ -594,9 +590,6 @@
             pltpu.VMEM((192, ff), BF),
             pltpu.VMEM((4 * nx, PACK, half_d), BF),
             pltpu.VMEM((n_exp, 2, PACK, half_d), BF),
-            pltpu.VMEM((n_tok, width), BF),
-            pltpu.VMEM((n_tok, width), BF),
-            pltpu.VMEM((192 * ff // 128, 128), F32),
             dma((4,)),
             dma((2,)),
             dma((2,)),
@@ -620,7 +613,7 @@
             dma((4 * nx,)),
             dma((2,)),
             dma((2,)),
-            dma((3,)),
+
         ],
         compiler_params=pltpu.CompilerParams(
             collective_id=0, has_side_effects=True, vmem_limit_bytes=56 * 2**20

time: 109 us -> 106 us (0.972)
  local copies, waits for them, and re-layouts: 5.13 us -> 3.1 us
    unnamed x7 -> x3, local copies, waits for them, and re-layouts: 5.13 us -> 3.1 us
where the time goes in v3:
time: 106 us
  Pallas kernels  103 us (97%)
  local copies, waits for them, and re-layouts  3.1 us (3%)
    pallas_call x1, Pallas kernels, layer(): pl.pallas_call(functools.partial(kernel, nx, nz), out_shape=(pltpu.VMEM((...  103 us
    unnamed x3, local copies, waits for them, and re-layouts  3.1 us

profile of v3, /device:TPU:1, one launch (start us, length us, event | category | flops | bytes accessed | tf_op | source)
XLA Modules:
  0.0 106.3 jit_solution(15023086274224795715)
XLA Ops:
  0.6 102.5 %shard_map.76 = (bf16[384,2048]{1,0:T(8,128)(2,1)S(1)}, bf16[384,2048]{1,0:T(8,128)(2,1)S(1)}, f32[1152,128]{1,0:T(8,128)S(1)}) custom-call(s32[8,384]{1,0:T(8,128)} %bitcast.8, s32[8,384]{1,0:T(8,128)} %bitcast.9, bf16[384,2048]{1,0:T(8,128)(2,1)} %tok_hbm.1, bf16[384,2048]{1,0:T(8,128)(2,1)} %og_hbm.1, bf16[192,768]{1,0:T(8,128)(2,1)} %bitcast.7), custom_call_target="tpu_custom_call" | custom-call | tf_op jit(solution)/shard_map/pallas_call | solution.py:558
  103.2 1.1 %copy.13 = bf16[384,2048]{1,0:T(8,128)(2,1)} copy(bf16[384,2048]{1,0:T(8,128)(2,1)S(1)} %get-tuple-element.15) | data formatting | bytes 3145728
  104.3 0.8 copy.15
  105.1 1.1 %copy.14 = bf16[384,2048]{1,0:T(8,128)(2,1)} copy(bf16[384,2048]{1,0:T(8,128)(2,1)S(1)} %get-tuple-element.16) | data formatting | bytes 3145728

commit v4 on v3

--- a/solution.py
+++ b/solution.py
@@ -371,12 +371,15 @@
             add_z(g, d, last, 2)
         reduce_yb(g).start()
 
-    def finish(g):
-        reduce_ya(g, 2 * hz - 1).wait_recv()
-        for s in (1, 0):
-            for d in (0, 1):
-                reduce_z(g, d, last, s).wait_recv()
-        reduce_yb(g).wait_recv()
+    def finish(g, s):
+        for d in (0, 1):
+            reduce_z(g, d, last, s).wait_recv()
+        if s == 0:
+            reduce_ya(g, 2 * hz - 1).wait_recv()
+            start, count, extra = 0, CUT, fin_ya
+        else:
+            reduce_yb(g).wait_recv()
+            start, count, extra = CUT, 192 - CUT, fin_yb
         lane_tiles = ff // 128
         first = group_tiles[g][0] * (LANES // 128)
 
@@ -396,14 +399,13 @@
 
         @pl.when(q == 0)
         def _():
-            total_rows(part.at[own(z)], CUT, 192 - CUT, fin_yb)
-            total_rows(part.at[own(z)], 0, CUT, fin_ya)
+            total_rows(part.at[own(z)], start, count, extra)
 
         @pl.when(q == 1)
         def _():
-            reduce_own(g).wait_recv()
-            total_rows(fin_own, CUT, 192 - CUT, fin_yb)
-            total_rows(fin_own, 0, CUT, fin_ya)
+            if s == 0:
+                reduce_own(g).wait_recv()
+            total_rows(fin_own, start, count, extra)
 
     def outputs(first, end):
         def step(n, carry):
@@ -512,13 +514,15 @@
         if t == hz - 1:
             finish_mates(1)
         pass_on(1, t, 0)
+    finish(0, 0)
 
     for j in range(1, n_peer):
         back_in(j).wait_recv()
     stay.wait()
     lax.fori_loop(0, 2 * tiles, combine, 0)
-    finish(0)
-    finish(1)
+    finish(0, 1)
+    finish(1, 0)
+    finish(1, 1)
 
     for g in (0, 1):
         for t in range(hz):

time: 106 us -> 106 us (level)
  no operation moved by 1% of the time
where the time goes in v4:
time: 106 us
  Pallas kernels  103 us (97%)
  local copies, waits for them, and re-layouts  3.1 us (3%)
    pallas_call x1, Pallas kernels, layer(): pl.pallas_call(functools.partial(kernel, nx, nz), out_shape=(pltpu.VMEM((...  103 us
    unnamed x3, local copies, waits for them, and re-layouts  3.1 us

profile of v4, /device:TPU:1, one launch (start us, length us, event | category | flops | bytes accessed | tf_op | source)
XLA Modules:
  0.0 106.3 jit_solution(8817265311548768845)
XLA Ops:
  0.6 102.5 %shard_map.76 = (bf16[384,2048]{1,0:T(8,128)(2,1)S(1)}, bf16[384,2048]{1,0:T(8,128)(2,1)S(1)}, f32[1152,128]{1,0:T(8,128)S(1)}) custom-call(s32[8,384]{1,0:T(8,128)} %bitcast.8, s32[8,384]{1,0:T(8,128)} %bitcast.9, bf16[384,2048]{1,0:T(8,128)(2,1)} %tok_hbm.1, bf16[384,2048]{1,0:T(8,128)(2,1)} %og_hbm.1, bf16[192,768]{1,0:T(8,128)(2,1)} %bitcast.7), custom_call_target="tpu_custom_call" | custom-call | tf_op jit(solution)/shard_map/pallas_call | solution.py:562
  103.2 1.1 %copy.13 = bf16[384,2048]{1,0:T(8,128)(2,1)} copy(bf16[384,2048]{1,0:T(8,128)(2,1)S(1)} %get-tuple-element.15) | data formatting | bytes 3145728
  104.3 0.8 copy.15
  105.1 1.1 %copy.14 = bf16[384,2048]{1,0:T(8,128)(2,1)} copy(bf16[384,2048]{1,0:T(8,128)(2,1)S(1)} %get-tuple-element.16) | data formatting | bytes 3145728
